TPU v7x, 256 devices: a whole 4x4x8 slice. The times are simulated.
256 devices in a mesh: seq: 64 (over y, z, core), ch: 4 (over x).
Axes of the slice: x: 4, y: 4, z: 8, core: 2. Of those that a mesh axis runs over, the one named last changes fastest.
Arguments:
- features: bfloat16 [3, 16384, 4096], P(None, 'seq', 'ch'), may hold values from -6 to 6
- short_taps: float32 [3, 3, 4096], P(None, None, 'ch'), may hold values from -3 to 3
- filter_taps: float32 [16384, 4096], P('seq', 'ch'), may hold values from -1.1 to 1.1, as said below
- skip_bias: float32 [4096], P('ch'), may hold values from -4 to 4
- out_weight: bfloat16 [4096, 4096], P('ch', 'seq'), may hold values from -0.09375 to 0.09375
Outputs:
- projected: bfloat16 [16384, 4096], P('seq', 'ch')
Inputs may be any that keep to these rules, and one draw needn't show every extreme that they name: `filter_taps`: the long filter's taps.
All inputs are finite; a program needn't handle non-finite values.
Results may differ from a plain program's by a relative error of at most 0.0049.
Values may be sent and summed in bfloat16 or wider, within the bound.
A program may use at most 128 MiB of HBM per device.

v0:
```python
import math

import jax
import jax.numpy as jnp
from jax import lax
from jax.sharding import PartitionSpec as P

highest = lax.Precision.HIGHEST


def from_behind(block, axis, distance):
    devices = range(lax.axis_size(axis))
    route = [(i - distance, i) for i in devices if i - distance in devices]
    return lax.ppermute(block, axis, route)


def wave_tables(row_count, col_count, period):
    row_index = lax.broadcasted_iota(jnp.int32, (row_count, col_count), 0)
    col_index = lax.broadcasted_iota(jnp.int32, (row_count, col_count), 1)
    phase_steps = row_index * col_index % period
    angles = phase_steps.astype(jnp.float32) * (2.0 * math.pi / period)
    return (jnp.cos(angles), jnp.sin(angles))


def dense_product(left_side, right_side):
    return jnp.dot(left_side, right_side, precision=highest, preferred_element_type=jnp.float32)


def block_forward(real_part, imag_part, tables):
    cos_table, sin_table = tables
    return (
        dense_product(cos_table, real_part) + dense_product(sin_table, imag_part),
        dense_product(cos_table, imag_part) - dense_product(sin_table, real_part),
    )


def block_inverse(real_part, imag_part, tables, factor):
    cos_table, sin_table = tables
    return (
        (dense_product(cos_table, real_part) - dense_product(sin_table, imag_part)) * factor,
        (dense_product(cos_table, imag_part) + dense_product(sin_table, real_part)) * factor,
    )


def spectral_product(first_pair, second_pair):
    return (
        first_pair[0] * second_pair[0] - first_pair[1] * second_pair[1],
        first_pair[0] * second_pair[1] + first_pair[1] * second_pair[0],
    )


def shards(features, short_taps, filter_taps, skip_bias, out_weight):
    row_count = features.shape[1]
    chan_width = features.shape[2]
    blocks = lax.axis_size("seq")
    fft_span = 2 * row_count
    rim_rows = features[:, row_count - 2 :, :]
    before = from_behind(rim_rows, "seq", 1)
    joined = jnp.concatenate([before, features], axis=1).astype(jnp.float32)
    mixed_rows = (
        short_taps[:, 0, None, :] * joined[:, 2:]
        + short_taps[:, 1, None, :] * joined[:, 1 : row_count + 1]
        + short_taps[:, 2, None, :] * joined[:, :row_count]
    )
    query_part = mixed_rows[0]
    gated_rows = mixed_rows[1] * mixed_rows[2]
    forward_tables = wave_tables(2 * blocks, blocks, 2 * blocks)
    inverse_tables = wave_tables(blocks, 2 * blocks, 2 * blocks)
    block_factor = 1.0 / (2 * blocks)
    freq_group = fft_span // blocks
    cos_local, sin_local = wave_tables(fft_span, row_count, fft_span)
    forward_local = jnp.concatenate([cos_local, -sin_local], axis=0)
    gated_spec = dense_product(forward_local, gated_rows).reshape(1, 2, fft_span, chan_width)
    filter_spec = dense_product(forward_local, filter_taps).reshape(1, 2, fft_span, chan_width)
    gated_parts, filter_parts = (
        lax.all_to_all(gated_spec, "seq", split_axis=2, concat_axis=0, tiled=True),
        lax.all_to_all(filter_spec, "seq", split_axis=2, concat_axis=0, tiled=True),
    )
    gated_pair = block_forward(
        gated_parts[:, 0].reshape(blocks, freq_group * chan_width),
        gated_parts[:, 1].reshape(blocks, freq_group * chan_width),
        forward_tables,
    )
    filter_pair = block_forward(
        filter_parts[:, 0].reshape(blocks, freq_group * chan_width),
        filter_parts[:, 1].reshape(blocks, freq_group * chan_width),
        forward_tables,
    )
    joint_real, joint_imag = spectral_product(gated_pair, filter_pair)
    back_real, back_imag = block_inverse(joint_real, joint_imag, inverse_tables, block_factor)
    outgoing = jnp.stack(
        [
            back_real.reshape(blocks, freq_group, chan_width),
            back_imag.reshape(blocks, freq_group, chan_width),
        ],
        axis=1,
    )
    returned = lax.all_to_all(outgoing, "seq", split_axis=0, concat_axis=2, tiled=True)
    cos_back, sin_back = wave_tables(fft_span, fft_span, fft_span)
    inverse_local = jnp.concatenate([cos_back, -sin_back], axis=1) * (1.0 / fft_span)
    series = dense_product(inverse_local, returned.reshape(2 * fft_span, chan_width))
    carried = from_behind(series[row_count:], "seq", 1)
    long_conv = series[:row_count] + carried
    hyena_out = (query_part * (long_conv + skip_bias[None, :] * gated_rows)).astype(jnp.bfloat16)
    partial_sums = jnp.dot(
        hyena_out,
        lax.all_gather(out_weight, "seq", axis=1, tiled=True),
        preferred_element_type=jnp.float32,
    )
    return lax.psum_scatter(partial_sums, "ch", scatter_dimension=1, tiled=True).astype(
        jnp.bfloat16
    )


def solution(mesh):
    placed = (P(None, "seq", "ch"), P(None, None, "ch"), P("seq", "ch"), P("ch"), P("ch", "seq"))
    return jax.shard_map(
        shards, mesh=mesh, in_specs=placed, out_specs=P("seq", "ch"), check_vma=False
    )
```

profile of v0, /device:TPU:1, one launch (start us, length us, event | category | flops | bytes accessed | tf_op | source)
XLA Modules:
  0.0 506.2 jit_solution(1848529365755154741)
XLA Ops:
  6.5 0.0 copy-start
  6.5 2.1 sine_negate_fusion.1
  8.6 0.0 copy-done
  8.6 3.8 fusion.113
  12.4 5.2 %copy.11 = f32[1,2,512,1024]{3,1,0,2:T(2,128)} copy(f32[1,2,512,1024]{3,2,1,0:T(8,128)S(1)} %bitcast.84) | data formatting | bytes 8388608 | tf_op jit(solution)/shard_map/reshape | solution.py:74
  17.5 13.5 %all-to-all-start.1 = ((f32[1,2,512,1024]{3,1,0,2:T(2,128)}), f32[1,2,512,1024]{3,1,0,2:T(2,128)}, u32[]{:S(2)}, u32[]{:S(2)}) async-start(f32[1,2,512,1024]{3,1,0,2:T(2,128)} %copy.11), calls=%async_computation.1 | async-start | bytes 8388608 | tf_op jit(solution)/shard_map/all_to_all | solution.py:77
  31.0 0.0 copy-start.6
  31.0 0.9 slice.49
  32.0 4.0 collective-permute-start
  36.0 0.0 copy-done.7
  36.0 0.1 pad_maximum_fusion.1
  36.1 82.8 %collective-permute-done = bf16[3,2,1024]{2,1,0:T(2,128)(2,1)S(1)} collective-permute-done((bf16[3,2,1024]{2,1,0:T(2,128)(2,1)S(1)}, bf16[3,2,1024]{2,1,0:T(2,128)(2,1)S(1)}, u32[]{:S(2)}, u32[]{:S(2)}) %collective-permute-start) | collective-permute-done | bytes 12320 | tf_op jit(solution)/shard_map/ppermute | solution.py:14
  118.9 0.0 copy-done.6
  118.9 0.5 maximum_convert_fusion
  119.4 0.9 fusion.2
  120.3 0.0 copy-start.4
  120.3 1.7 copy-done.4
  122.0 3.8 convolution_bitcast_fusion
  125.8 5.2 %copy.10 = f32[1,2,512,1024]{3,1,0,2:T(2,128)} copy(f32[1,2,512,1024]{3,2,1,0:T(8,128)S(1)} %convolution_bitcast_fusion) | data formatting | bytes 8388608 | tf_op jit(solution)/shard_map/dot_general | solution.py:26
  131.0 0.0 all-to-all-done.1
  131.0 13.8 %all-to-all-start = ((f32[1,2,512,1024]{3,1,0,2:T(2,128)}), f32[1,2,512,1024]{3,1,0,2:T(2,128)}, u32[]{:S(2)}, u32[]{:S(2)}) async-start(f32[1,2,512,1024]{3,1,0,2:T(2,128)} %copy.10), calls=%async_computation | async-start | bytes 8388608 | tf_op jit(solution)/shard_map/all_to_all | solution.py:76
  144.9 0.0 all-gather.2.cloned.1.call-start
  144.9 0.7 all-gather.2.cloned.1.call-update
  145.6 14.6 %slice_reduce_fusion = (f32[64,8,1024]{2,1,0:T(8,128)S(1)}, f32[64,8,1024]{2,1,0:T(8,128)S(1)}) fusion(f32[64,2,8,1024]{3,1,2,0:T(2,128)} %bitcast.13), kind=kLoop, calls=%fused_computation.17 | loop fusion | bytes 8388608 | tf_op jit(solution)/shard_map/slice | solution.py:86
  160.2 1.2 copy.20
  161.4 1.2 copy.21
  162.6 3.8 fusion.44
  166.3 3.8 fusion.40
  170.1 5.6 %convolution_add_fusion = f32[128,8192]{1,0:T(8,128)} fusion(f32[128,8192]{1,0:T(8,128)S(1)} %fusion.44, f32[64,8192]{1,0:T(8,128)S(1)} %bitcast.78), kind=kOutput, calls=%fused_computation.2 | convolution fusion | flops 806469632 | bytes 10485760 | tf_op jit(solution)/shard_map/dot_general | solution.py:26
  175.7 6.0 %convolution_subtract_fusion = f32[128,8192]{1,0:T(8,128)} fusion(f32[128,8192]{1,0:T(8,128)S(1)} %fusion.40, f32[64,8192]{1,0:T(8,128)S(1)} %bitcast.76), kind=kOutput, calls=%fused_computation | convolution fusion | flops 806469632 | bytes 10485760 | tf_op jit(solution)/shard_map/dot_general | solution.py:26
  181.7 79.7 %all-to-all-done = f32[1,2,512,1024]{3,1,0,2:T(2,128)} async-done(((f32[1,2,512,1024]{3,1,0,2:T(2,128)}), f32[1,2,512,1024]{3,1,0,2:T(2,128)}, u32[]{:S(2)}, u32[]{:S(2)}) %all-to-all-start) | async-done | bytes 4194336 | tf_op jit(solution)/shard_map/all_to_all | solution.py:76
  261.4 14.2 %slice_reduce_fusion.3 = (f32[64,8,1024]{2,1,0:T(8,128)S(1)}, f32[64,8,1024]{2,1,0:T(8,128)S(1)}) fusion(f32[64,2,8,1024]{3,1,2,0:T(2,128)} %bitcast.7), kind=kLoop, calls=%fused_computation.20 | loop fusion | bytes 8388608 | tf_op jit(solution)/shard_map/slice | solution.py:80
  275.5 1.2 copy.18
  276.7 1.2 copy.19
  278.0 3.8 fusion.46
  281.7 3.7 fusion.42
  285.4 0.0 copy-start.2
  285.4 0.0 copy-start.3
  285.4 5.6 %convolution_add_fusion.1 = f32[128,8192]{1,0:T(8,128)} fusion(f32[128,8192]{1,0:T(8,128)S(1)} %fusion.46, f32[64,8192]{1,0:T(8,128)S(1)} %bitcast.80), kind=kOutput, calls=%fused_computation.3 | convolution fusion | flops 806469632 | bytes 10485760 | tf_op jit(solution)/shard_map/dot_general | solution.py:26
  291.0 0.0 copy-done.2
  291.0 6.8 %multiply_subtract_fusion = (f32[128,8192]{1,0:T(8,128)S(1)}, f32[128,8192]{1,0:T(8,128)S(1)}) fusion(f32[128,8192]{1,0:T(8,128)S(1)} %copy-done.3, f32[128,8192]{1,0:T(8,128)} %convolution_add_fusion.1, f32[128,8192]{1,0:T(8,128)S(1)} %copy-done.2, f32[128,8192]{1,0:T(8,128)S(1)} %fusion.42, f32[64,8192]{1,0:T(8,128)S(1)} %bitcast.82), kind=kOutput, calls=%fused_computation.10 | convolution fusion | flops 812761088 | bytes 27262976 | tf_op jit(solution)/shard_map/dot_general | solution.py:26
  297.8 2.4 fusion.59
  300.3 2.6 fusion.1
  302.9 1.2 copy.22
  304.1 2.4 fusion.57
  306.5 2.6 fusion
  309.1 1.4 copy.23
  310.5 2.2 pad_maximum_fusion
  312.8 6.5 %all-to-all-start.2 = ((f32[64,2,8,1024]{3,2,1,0:T(8,128)}), f32[64,2,8,1024]{3,2,1,0:T(8,128)}, u32[]{:S(2)}, u32[]{:S(2)}) async-start(f32[64,2,8,1024]{3,2,1,0:T(8,128)} %pad_maximum_fusion), calls=%async_computation.2 | async-start | bytes 8388608 | tf_op jit(solution)/shard_map/all_to_all | solution.py:98
  319.2 0.0 reduce-scatter.2.cloned.1.call-start
  319.3 5.3 %sine_negate_fusion = (f32[512,512]{1,0:T(8,128)S(1)}, f32[512,512]{1,0:T(8,128)}) fusion(), kind=kLoop, calls=%fused_computation.42 | loop fusion | flops 3932160 | bytes 2097152 | tf_op jit(solution)/shard_map/neg | solution.py:100
  324.6 90.5 %all-to-all-done.2 = f32[64,2,8,1024]{3,2,1,0:T(8,128)} async-done(((f32[64,2,8,1024]{3,2,1,0:T(8,128)}), f32[64,2,8,1024]{3,2,1,0:T(8,128)}, u32[]{:S(2)}, u32[]{:S(2)}) %all-to-all-start.2) | async-done | bytes 4194336 | tf_op jit(solution)/shard_map/all_to_all | solution.py:98
  415.1 2.6 copy.14
  417.7 0.0 copy-start.8
  417.7 6.9 %fusion.4 = f32[512,1024]{1,0:T(8,128)S(1)} fusion(f32[1024,1024]{1,0:T(8,128)S(1)} %bitcast.83, f32[512,512]{1,0:T(8,128)S(1)} %get-tuple-element.18, f32[512,512]{1,0:T(8,128)S(1)} %copy-done.5), kind=kOutput, calls=%fused_computation.22 | convolution fusion | flops 6443499520 | bytes 8388608 | tf_op jit(solution)/shard_map/dot_general | solution.py:26
  424.6 0.1 slice.75
  424.7 1.9 collective-permute-start.1
  426.6 0.0 all-gather.2.cloned.1.call-done
  426.6 11.7 %collective-permute-done.1 = f32[256,1024]{1,0:T(8,128)} collective-permute-done((f32[256,1024]{1,0:T(8,128)S(1)}, f32[256,1024]{1,0:T(8,128)}, u32[]{:S(2)}, u32[]{:S(2)}) %collective-permute-start.1) | collective-permute-done | bytes 1048608 | tf_op jit(solution)/shard_map/ppermute | solution.py:14
  438.3 0.0 copy-done.8
  438.3 9.2 %fusion.21 = f32[256,4096]{1,0:T(8,128)} fusion(bf16[1024,4096]{0,1:T(8,128)(2,1)} %all-gather.2.cloned.1.call-done, f32[256,1024]{1,0:T(8,128)} %collective-permute-done.1, f32[512,1024]{1,0:T(8,128)S(1)} %fusion.4, f32[3,256,1024]{2,1,0:T(8,128)} %copy-done.4, f32[1024]{0:T(1024)S(1)} %copy-done.8), kind=kOutput, calls=%fused_computation.52 | convolution fusion | flops 2149056512 | bytes 17829888 | tf_op jit(solution)/shard_map/dot_general | solution.py:105
  447.5 0.0 reduce-scatter.2.cloned.1.call-update
  447.6 49.5 %reduce-scatter.2.cloned.1.call-done = f32[256,1024]{1,0:T(8,128)} async-done(((f32[256,4096]{1,0:T(8,128)}), f32[256,1024]{1,0:T(8,128)}) %reduce-scatter.2.cloned.1.call-update) | async-done | bytes 1048592 | tf_op jit(solution)/shard_map/reduce_scatter | solution.py:110
  497.1 2.1 convert_element_type.51
  (9 shorter events, 0.1 us)
Async XLA Ops:
  6.5 2.1 copy-start
  17.5 18.4 %copy-start.7 = (f32[3,3,1024]{2,1,0:T(4,128)S(1)}, f32[3,3,1024]{2,1,0:T(4,128)}, u32[]{:S(2)}) copy-start(f32[3,3,1024]{2,1,0:T(4,128)} %param.6) | copy-start | bytes 110596
  17.5 113.5 %all-to-all-start.1 = ((f32[1,2,512,1024]{3,1,0,2:T(2,128)}), f32[1,2,512,1024]{3,1,0,2:T(2,128)}, u32[]{:S(2)}, u32[]{:S(2)}) async-start(f32[1,2,512,1024]{3,1,0,2:T(2,128)} %copy.11), calls=%async_computation.1 | async-start | bytes 8388608 | tf_op jit(solution)/shard_map/all_to_all | solution.py:77
  31.0 87.9 %copy-start.6 = (bf16[3,256,1024]{2,1,0:T(8,128)(2,1)S(1)}, bf16[3,256,1024]{2,1,0:T(8,128)(2,1)}, u32[]{:S(2)}) copy-start(bf16[3,256,1024]{2,1,0:T(8,128)(2,1)} %param.5) | copy-start | bytes 4718596
  32.0 86.9 %collective-permute-start = (bf16[3,2,1024]{2,1,0:T(2,128)(2,1)S(1)}, bf16[3,2,1024]{2,1,0:T(2,128)(2,1)S(1)}, u32[]{:S(2)}, u32[]{:S(2)}) collective-permute-start(bf16[3,2,1024]{2,1,0:T(2,128)(2,1)S(1)} %slice.49), channel_id=1, source_target_pairs={{0,4},{4,8},{8,12},{12,16},{16,20},{20,24},{24,28},{28,32},{32,36}... | collective-permute-start | bytes 36872 | tf_op jit(solution)/shard_map/ppermute | solution.py:14
  120.3 1.7 copy-start.4
  131.0 130.3 %all-to-all-start = ((f32[1,2,512,1024]{3,1,0,2:T(2,128)}), f32[1,2,512,1024]{3,1,0,2:T(2,128)}, u32[]{:S(2)}, u32[]{:S(2)}) async-start(f32[1,2,512,1024]{3,1,0,2:T(2,128)} %copy.10), calls=%async_computation | async-start | bytes 8388608 | tf_op jit(solution)/shard_map/all_to_all | solution.py:76
  144.9 281.8 %all-gather.2.cloned.1.call-start = ((), (), s32[]{:S(2)}) async-start(), calls=%async_computation.4 | async-start | bytes 8519680 | tf_op jit(solution)/shard_map/all_gather | solution.py:107
  285.4 5.6 %copy-start.2 = (f32[128,8192]{1,0:T(8,128)S(1)}, f32[128,8192]{1,0:T(8,128)}, u32[]{:S(2)}) copy-start(f32[128,8192]{1,0:T(8,128)} %convolution_add_fusion) | copy-start | bytes 12582916
  285.4 5.6 %copy-start.3 = (f32[128,8192]{1,0:T(8,128)S(1)}, f32[128,8192]{1,0:T(8,128)}, u32[]{:S(2)}) copy-start(f32[128,8192]{1,0:T(8,128)} %convolution_subtract_fusion) | copy-start | bytes 12582916
  312.8 102.4 %all-to-all-start.2 = ((f32[64,2,8,1024]{3,2,1,0:T(8,128)}), f32[64,2,8,1024]{3,2,1,0:T(8,128)}, u32[]{:S(2)}, u32[]{:S(2)}) async-start(f32[64,2,8,1024]{3,2,1,0:T(8,128)} %pad_maximum_fusion), calls=%async_computation.2 | async-start | bytes 8388608 | tf_op jit(solution)/shard_map/all_to_all | solution.py:98
  319.2 177.8 %reduce-scatter.2.cloned.1.call-start = ((), (), s32[]{:S(2)}) async-start(), calls=%async_computation.5 | async-start | bytes 5242880 | tf_op jit(solution)/shard_map/reduce_scatter | solution.py:110
  415.1 2.6 copy-start.5
  417.7 20.6 %copy-start.8 = (f32[1024]{0:T(1024)S(1)}, f32[1024]{0:T(1024)}, u32[]{:S(2)}) copy-start(f32[1024]{0:T(1024)} %param.8) | copy-start | bytes 12292
  424.7 13.7 %collective-permute-start.1 = (f32[256,1024]{1,0:T(8,128)S(1)}, f32[256,1024]{1,0:T(8,128)}, u32[]{:S(2)}, u32[]{:S(2)}) collective-permute-start(f32[256,1024]{1,0:T(8,128)S(1)} %slice.75), channel_id=1, source_target_pairs={{0,4},{4,8},{8,12},{12,16},{16,20},{20,24},{24,28},{28,32},{32,36}... | collective-permute-start | bytes 3145736 | tf_op jit(solution)/shard_map/ppermute | solution.py:14
  438.3 60.8 %copy-start.1 = (f32[256,1024]{1,0:T(8,128)S(1)}, f32[256,1024]{1,0:T(8,128)}, u32[]{:S(2)}) copy-start(f32[256,1024]{1,0:T(8,128)} %param.7) | copy-start | bytes 3145732
Sparse Core Ops, SparseCore 0:
  148.5 117.0 all-gather.1
  447.7 49.3 reduce-scatter.1
where the time goes:
time: 514 us; the launch traced here: 506 us
  waiting for transfers between devices  315 us (61%)
  matrix products  72.6 us (14%)
  local copies, waits for them, and re-layouts  51.8 us (10%)
  starting transfers between devices  39.8 us (8%)
  between operations  14 us (3%)
  other arithmetic  13.2 us (3%)
    ppermute x2, waiting for transfers between devices, from_behind(): return lax.ppermute(block, axis, route)  94.5 us
    all_to_all x1, waiting for transfers between devices, shards(): lax.all_to_all(outgoing, 'seq', split_axis=0, concat_axis=2, tiled=True)  90.5 us
    all_to_all x1, waiting for transfers between devices, shards(): lax.all_to_all(gated_spec, 'seq', split_axis=2, concat_axis=0, tiled=True)  79.7 us
    dot_general x15, matrix products, dense_product(): jnp.dot(left_side, right_side, precision=highest, preferred_element_type=...  63.4 us
    reduce_scatter x1, waiting for transfers between devices, shards(): lax.psum_scatter(partial_sums, 'ch', scatter_dimension=1, tiled=True)  49.5 us
    slice x1, local copies, waits for them, and re-layouts, shards(): filter_parts[:, 1].reshape(blocks, freq_group * chan_width)  14.6 us
    slice x1, local copies, waits for them, and re-layouts, shards(): gated_parts[:, 0].reshape(blocks, freq_group * chan_width)  14.2 us
    all_to_all x1, starting transfers between devices, shards(): lax.all_to_all(gated_spec, 'seq', split_axis=2, concat_axis=0, tiled=True)  13.8 us
  transfers between devices with their start and end apart: 7, of which 5 were waited for; matrix products, arithmetic and copies ran while one was open for 22% of the time, Pallas kernels for 0%

commit v1 on v0

v1 whole, which is shorter than its diff:
```python
import functools
import math

import jax
import jax.numpy as jnp
import numpy as np
from jax import lax
from jax.experimental import pallas as pl
from jax.experimental.pallas import tpu as pltpu
from jax.sharding import PartitionSpec as P

MESH = pl.DeviceIdType.MESH
f32, bf16 = jnp.float32, jnp.bfloat16

BLOCKS = 64
ROWS = 256
CHAN = 1024
SHARE = CHAN // BLOCKS
POINTS = 2 * BLOCKS * ROWS
HALF = BLOCKS + 1
PADDED = 80
GROUP = 4


def split_np(table):
    high = np.asarray(table, np.float32).astype(jnp.bfloat16)
    low = (np.asarray(table, np.float64) - high.astype(np.float64)).astype(jnp.bfloat16)
    return high, low


@functools.lru_cache(maxsize=None)
def fourier_tables():
    outer = 2 * np.pi * np.outer(np.arange(HALF), np.arange(BLOCKS)) / (2 * BLOCKS)
    block_forward = np.zeros((2 * PADDED, BLOCKS))
    block_forward[:HALF] = np.cos(outer)
    block_forward[PADDED : PADDED + HALF] = -np.sin(outer)
    weight = np.full((HALF, 1), 2.0 / POINTS)
    weight[0] = weight[-1] = 1.0 / POINTS
    block_inverse = np.zeros((BLOCKS, 2 * PADDED))
    block_inverse[:, :HALF] = (np.cos(outer) * weight).T
    block_inverse[:, PADDED : PADDED + HALF] = -(np.sin(outer) * weight).T
    twist = 2 * np.pi * np.outer(np.arange(PADDED), np.arange(ROWS)) / POINTS
    inner = 2 * np.pi * (np.outer(np.arange(ROWS), np.arange(ROWS)) % ROWS) / ROWS
    cos_in, sin_in = np.cos(inner), np.sin(inner)
    row_forward = np.block([[cos_in, -sin_in], [sin_in, cos_in]])
    row_inverse = np.block([[cos_in, sin_in], [-sin_in, cos_in]])
    return (
        *split_np(block_forward),
        *split_np(block_inverse),
        *split_np(row_forward),
        *split_np(row_inverse),
        np.cos(twist).astype(np.float32),
        np.sin(twist).astype(np.float32),
    )


def split(value):
    high = value.astype(bf16)
    return high, (value - high.astype(f32)).astype(bf16)


def dot(left, right):
    return jnp.dot(left, right, preferred_element_type=f32)


def dot_wide(left, right_high, right_low):
    high, low = split(left)
    return dot(high, right_high) + (dot(high, right_low) + dot(low, right_high))


def kernel(
    feat, taps, filt, skip, weight,
    bf_hi, bf_lo, bi_hi, bi_lo, rf_hi, rf_lo, ri_hi, ri_lo, tw_cos, tw_sin,
    out,
    halo, f_out, g_out, y_out, f_in, g_in, y_in, wide, spec, query, gated, w_own, w_all, hyena, acc,
    halo_sems, f_sems, g_sems, y_sems, t_sems, z_send, z_recv, v_send, v_recv, p_send, p_recv, h_send, h_recv,
):
    me = lax.axis_index("seq")
    col = lax.axis_index("ch")
    row = lax.div(me, 16)
    deep = lax.div(lax.rem(me, 16), 2)
    core = lax.rem(me, 2)

    def seq_at(r, d, c):
        return (r * 8 + d) * 2 + c

    def wrap(i, n):
        return lax.rem(i + n, n)

    def remote(src, dst, send, recv, **where):
        return pltpu.make_async_remote_copy(
            src_ref=src, dst_ref=dst, send_sem=send, recv_sem=recv, device_id=where, device_id_type=MESH
        )

    barrier = pltpu.get_barrier_semaphore()

    def greet(k, carry):
        pl.semaphore_signal(
            barrier, inc=1, device_id={"seq": lax.rem(me + k, BLOCKS)}, device_id_type=MESH
        )
        return carry

    lax.fori_loop(1, BLOCKS, greet, 0)
    for step in (1, 3):
        pl.semaphore_signal(barrier, inc=1, device_id={"ch": lax.rem(col + step, 4)}, device_id_type=MESH)
    mirror = {"seq": seq_at(col, deep, core), "ch": row}

    @pl.when(row != col)
    def _():
        pl.semaphore_signal(barrier, inc=1, device_id=mirror, device_id_type=MESH)

    pl.semaphore_wait(barrier, BLOCKS + 1 + (row != col).astype(jnp.int32))

    halo_copy = remote(
        feat.at[:, pl.ds(ROWS - 16, 16), :], halo, halo_sems.at[0], halo_sems.at[1],
        seq=lax.rem(me + 1, BLOCKS),
    )
    halo_copy.start()

    w_own[...] = weight[...].astype(f32).T.astype(bf16)
    mirror_copy = remote(w_own, w_all.at[col, deep, core], t_sems.at[0], t_sems.at[1], **mirror)

    @pl.when(row != col)
    def _():
        mirror_copy.start()

    @pl.when(row == col)
    def _():
        w_all[row, deep, core] = w_own[...]

    def exchange(src, dst, sems):
        def send(k, carry):
            to = lax.rem(me + k * STRIDE, BLOCKS)
            remote(
                src.at[pl.ds(pl.multiple_of(to * SHARE, SHARE), SHARE)],
                dst.at[pl.ds(pl.multiple_of(me * SHARE, SHARE), SHARE)],
                sems.at[0], sems.at[1], seq=to,
            ).start()
            return carry

        lax.fori_loop(1, BLOCKS, send, 0)
        here = pl.ds(pl.multiple_of(me * SHARE, SHARE), SHARE)
        dst[here, :] = src[here, :]

    def exchanged(src, dst, sems):
        others = pl.ds(0, (BLOCKS - 1) * SHARE)
        pltpu.make_async_copy(src.at[others], dst.at[others], sems.at[1]).wait()
        pltpu.make_async_copy(src.at[others], dst.at[others], sems.at[0]).wait()

    f_out[...] = filt[...].T.astype(bf16)
    exchange(f_out, f_in, f_sems)

    def z_copies(i):
        rows = (pl.ds(0, 64), pl.ds(0, 64)) if i < 3 else (pl.ds(0, 32), pl.ds(32, 32))
        up, down = wrap(deep - i, 8), lax.rem(deep + i, 8)
        return (
            remote(
                w_all.at[row, up, core, rows[0]], w_all.at[row, up, core, rows[0]],
                z_send.at[0, i], z_recv.at[0, i], seq=seq_at(row, lax.rem(deep + 1, 8), core),
            ),
            remote(
                w_all.at[row, down, core, rows[1]], w_all.at[row, down, core, rows[1]],
                z_send.at[1, i], z_recv.at[1, i], seq=seq_at(row, lax.rem(deep + 7, 8), core),
            ),
        )

    @pl.when(row != col)
    def _():
        mirror_copy.wait()

    z_steps = [z_copies(i) for i in range(4)]
    for copy in z_steps[0]:
        copy.start()

    halo_copy.wait()
    first = (me != 0).astype(f32)

    def mixed(b):
        rows = feat[b].astype(f32)
        edge = halo[b].astype(f32) * first
        joined = jnp.concatenate([edge[8:16], rows], axis=0)
        back_one = pltpu.roll(joined, 1, 0)[8:]
        back_two = pltpu.roll(joined, 2, 0)[8:]
        return taps[b, 0:1] * rows + taps[b, 1:2] * back_one + taps[b, 2:3] * back_two

    gated[...] = mixed(1) * mixed(2)
    g_out[...] = gated[...].T.astype(bf16)
    exchange(g_out, g_in, g_sems)
    query[...] = mixed(0)

    for i in range(1, 4):
        for copy, later in zip(z_steps[i - 1], z_steps[i]):
            copy.wait_recv()
            later.start()
    for copy in z_steps[3]:
        copy.wait_recv()

    def v_copy(direction, part, source, low, n):
        ref = w_all.at[source, pl.ds(low, n), core]
        to = lax.rem(row + (1 if direction == 0 else 3), 4)
        return remote(
            ref, ref, v_send.at[direction, part], v_recv.at[direction, part], seq=seq_at(to, deep, core)
        )

    before, after = wrap(row - 1, 4), lax.rem(row + 1, 4)
    v_up = [v_copy(0, 0, row, 0, 4), v_copy(0, 1, row, 4, 4), v_copy(0, 2, before, 0, 4)]
    v_down = [v_copy(1, 0, row, 4, 4), v_copy(1, 1, row, 0, 4), v_copy(1, 2, after, 4, 4)]
    for part in (0, 1):
        v_up[part].start()
        v_down[part].start()

    def p_copy(i):
        ref = w_all.at[lax.rem(row + i, 4), :, core]
        return remote(ref, ref, p_send.at[i], p_recv.at[i], seq=seq_at(row, deep, 1 - core))

    p_copies = [p_copy(i) for i in range(4)]
    p_copies[0].start()

    def widen(received):
        wide[0] = received[:, :128].astype(f32)
        wide[1] = received[:, 128:].astype(f32)

    def spectra(q):
        lines = []
        for c in range(GROUP):
            every = pl.ds(q * GROUP + c, BLOCKS, stride=SHARE)
            line = jnp.concatenate([wide[0, every, :], wide[1, every, :]], axis=1).astype(bf16)
            both = dot(bf_hi[...], line) + dot(bf_lo[...], line)
            real, imag = both[:PADDED], both[PADDED:]
            lines.append(
                jnp.concatenate(
                    [
                        real * tw_cos[...] + imag * tw_sin[...],
                        imag * tw_cos[...] - real * tw_sin[...],
                    ],
                    axis=1,
                )
            )
        return dot_wide(jnp.concatenate(lines, axis=0), rf_hi[...], rf_lo[...])

    exchanged(f_out, f_in, f_sems)
    widen(f_in)

    def filter_group(q, carry):
        spec[q] = spectra(q)
        return carry

    lax.fori_loop(0, SHARE // GROUP, filter_group, 0)

    v_up[0].wait_recv()
    v_up[2].start()
    v_down[0].wait_recv()
    v_down[2].start()

    exchanged(g_out, g_in, g_sems)
    widen(g_in)

    def conv_group(q, carry):
        signal = spectra(q)
        taps_spec = spec[q]
        sr, si = signal[:, :ROWS], signal[:, ROWS:]
        tr, ti = taps_spec[:, :ROWS], taps_spec[:, ROWS:]
        joint = jnp.concatenate([sr * tr - si * ti, sr * ti + si * tr], axis=1)
        back = dot_wide(joint, ri_hi[...], ri_lo[...])
        for c in range(GROUP):
            real = back[c * PADDED : (c + 1) * PADDED, :ROWS]
            imag = back[c * PADDED : (c + 1) * PADDED, ROWS:]
            both = jnp.concatenate(
                [
                    real * tw_cos[...] - imag * tw_sin[...],
                    imag * tw_cos[...] + real * tw_sin[...],
                ],
                axis=0,
            )
            high, low = split(both)
            series = dot(bi_hi[...], high) + (dot(bi_hi[...], low) + dot(bi_lo[...], high))
            every = pl.ds(q * GROUP + c, BLOCKS, stride=SHARE)
            wide[0, every, :] = series[:, :128]
            wide[1, every, :] = series[:, 128:]
        return carry

    lax.fori_loop(0, SHARE // GROUP, conv_group, 0)
    y_out[:, :128] = wide[0].astype(bf16)
    y_out[:, 128:] = wide[1].astype(bf16)
    exchange(y_out, y_in, y_sems)

    v_up[1].wait_recv()
    p_copies[3].start()
    v_down[1].wait_recv()
    p_copies[1].start()
    v_up[2].wait_recv()
    v_down[2].wait_recv()
    p_copies[2].start()

    exchanged(y_out, y_in, y_sems)
    long_conv = y_in[...].astype(f32).T
    hyena[col] = (query[...] * (long_conv + skip[...] * gated[...])).astype(bf16)

    def h_copy(direction, part, source, low):
        ref = hyena.at[source, pl.ds(low, 128)]
        to = lax.rem(col + (1 if direction == 0 else 3), 4)
        return remote(ref, ref, h_send.at[direction, part], h_recv.at[direction, part], ch=to)

    left, right = wrap(col - 1, 4), lax.rem(col + 1, 4)
    h_up = [h_copy(0, 0, col, 0), h_copy(0, 1, col, 128), h_copy(0, 2, left, 0)]
    h_down = [h_copy(1, 0, col, 128), h_copy(1, 1, col, 0), h_copy(1, 2, right, 128)]
    for part in (0, 1):
        h_up[part].start()
        h_down[part].start()
    for copy in p_copies:
        copy.wait_recv()

    def project(source, start):
        def tile(j, carry):
            cols = pl.ds(pl.multiple_of(j * 256, 256), 256)
            block = w_all[source, pl.ds(2 * j, 2)].reshape(256, CHAN)
            part = lax.dot_general(
                hyena[source], block, (((1,), (1,)), ((), ())), preferred_element_type=f32
            )
            acc[:, cols] = part if start else acc[:, cols] + part
            return carry

        lax.fori_loop(0, 4, tile, 0)

    h_up[0].wait_recv()
    h_up[2].start()
    h_down[0].wait_recv()
    h_down[2].start()
    project(col, True)
    h_up[1].wait_recv()
    project(left, False)
    h_down[1].wait_recv()
    project(right, False)
    h_up[2].wait_recv()
    h_down[2].wait_recv()
    project(lax.rem(col + 2, 4), False)
    out[...] = acc[...].astype(bf16)

    for copies in (*z_steps, v_up, v_down, p_copies, h_up, h_down):
        for copy in copies:
            copy.wait_send()


STRIDE = 1


def shards(features, short_taps, filter_taps, skip_bias, out_weight):
    tables = [jnp.asarray(t) for t in fourier_tables()]
    whole = pl.BlockSpec(memory_space=pltpu.VMEM)
    dma = pltpu.SemaphoreType.DMA
    return pl.pallas_call(
        kernel,
        out_shape=jax.ShapeDtypeStruct((ROWS, CHAN), bf16),
        in_specs=[whole] * (5 + len(tables)),
        out_specs=whole,
        scratch_shapes=[
            pltpu.VMEM((3, 16, CHAN), bf16),
            *[pltpu.VMEM((CHAN, ROWS), bf16)] * 6,
            pltpu.VMEM((2, CHAN, 128), f32),
            pltpu.VMEM((SHARE // GROUP, GROUP * PADDED, 2 * ROWS), f32),
            pltpu.VMEM((ROWS, CHAN), f32),
            pltpu.VMEM((ROWS, CHAN), f32),
            pltpu.VMEM((BLOCKS, CHAN), bf16),
            pltpu.VMEM((4, 8, 2, 64, CHAN), bf16),
            pltpu.VMEM((4, ROWS, CHAN), bf16),
            pltpu.VMEM((ROWS, CHAN), f32),
            *[dma((2,))] * 5,
            dma((2, 4)), dma((2, 4)),
            dma((2, 3)), dma((2, 3)),
            dma((4,)), dma((4,)),
            dma((2, 3)), dma((2, 3)),
        ],
        compiler_params=pltpu.CompilerParams(
            collective_id=0, has_side_effects=True, vmem_limit_bytes=60 * 1024 * 1024
        ),
    )(features, short_taps, filter_taps, skip_bias[None, :], out_weight, *tables)


def solution(mesh):
    placed = (P(None, "seq", "ch"), P(None, None, "ch"), P("seq", "ch"), P("ch"), P("ch", "seq"))
    return jax.shard_map(
        shards, mesh=mesh, in_specs=placed, out_specs=P("seq", "ch"), check_vma=False
    )
```

time: 514 us -> 120 us (0.23); the launches traced: 506 us -> 120 us
  waiting for transfers between devices: 315 us -> 0 us
  Pallas kernels: 0 us -> 116 us
  matrix products: 72.6 us -> 0 us
  local copies, waits for them, and re-layouts: 51.8 us -> 3.61 us
  starting transfers between devices: 39.8 us -> 0 us
  between operations: 14 us -> 0.01 us
  other arithmetic: 13.2 us -> 0 us
    all_to_all x3 -> x0, waiting for transfers between devices: 170 us -> none  [the longest x1 90.5 us: shards(): lax.all_to_all(outgoing, 'seq', split_axis=0, concat_axis=2, tiled=True)]
    pallas_call x0 -> x1, Pallas kernels: none -> 116 us  [shards(): pl.pallas_call(kernel, out_shape=jax.ShapeDtypeStruct((ROWS, CHAN), bf16)...]
    ppermute x2 -> x0, waiting for transfers between devices: 94.5 us -> none  [from_behind(): return lax.ppermute(block, axis, route)]
    dot_general x16 -> x0, matrix products: 72.6 us -> none  [the longest x15 63.4 us: dense_product(): jnp.dot(left_side, right_side, precision=highest, preferred_element_type=...]
    reduce_scatter x1 -> x0, waiting for transfers between devices: 49.5 us -> none  [shards(): lax.psum_scatter(partial_sums, 'ch', scatter_dimension=1, tiled=True)]
    all_to_all x3 -> x0, starting transfers between devices: 33.8 us -> none  [the longest x1 13.8 us: shards(): lax.all_to_all(gated_spec, 'seq', split_axis=2, concat_axis=0, tiled=True)]
    slice x5 -> x0, local copies, waits for them, and re-layouts: 29.7 us -> none  [the longest x1 14.6 us: shards(): filter_parts[:, 1].reshape(blocks, freq_group * chan_width)]
    neg x2 -> x0, other arithmetic: 7.38 us -> none  [the longest x1 5.31 us: shards(): -sin_back]
  transfers between devices with their start and end apart: 7 -> 0, of which waited for: 5 -> 0; matrix products, arithmetic and copies ran while one was open for 22% -> 0% of each run, Pallas kernels for 0% -> 0%
where the time goes in v1:
time: 120 us
  Pallas kernels  116 us (97%)
  local copies, waits for them, and re-layouts  3.61 us (3%)
    pallas_call x1, Pallas kernels, shards(): pl.pallas_call(kernel, out_shape=jax.ShapeDtypeStruct((ROWS, CHAN), bf16)...  116 us
    unnamed x2, local copies, waits for them, and re-layouts  3.61 us

profile of v1, /device:TPU:1, one launch (start us, length us, event | category | flops | bytes accessed | tf_op | source)
XLA Modules:
  0.0 119.9 jit_solution(11637847156281507090)
XLA Ops:
  0.0 1.7 %copy.16.weight = bf16[1024,64]{1,0:T(8,128)(2,1)} copy(bf16[1024,64]{0,1:T(8,128)(2,1)} %param.19) | data formatting | bytes 262144 | tf_op args[4]
  1.7 116.3 %shard_map.145 = bf16[256,1024]{1,0:T(8,128)(2,1)} custom-call(bf16[3,256,1024]{2,1,0:T(8,128)(2,1)} %feat.1, f32[3,3,1024]{2,1,0:T(4,128)} %taps.1, f32[256,1024]{1,0:T(8,128)} %filt.1, f32[1,1024]{1,0:T(1,128)} %bitcast.1, bf16[1024,64]{1,0:T(8,128)(2,1)} %copy.16.weight, bf16[160,64]{1,0:T(8,128)(2,1)} %constant.20.clone.bf_hi, ...), custom_call_target="tpu_custom_call" | custom-call | tf_op jit(solution)/shard_map/pallas_call | solution.py:351
  118.0 1.9 %copy.18 = bf16[256,1024]{1,0:T(8,128)(2,1)} copy(bf16[256,1024]{1,0:T(8,128)(2,1)} %shard_map.145) | data formatting | bytes 1048576

commit v2 on v1

v2 whole, which is shorter than its diff:
```python
import functools
import math

import jax
import jax.numpy as jnp
import numpy as np
from jax import lax
from jax.experimental import pallas as pl
from jax.experimental.pallas import tpu as pltpu
from jax.sharding import PartitionSpec as P

MESH = pl.DeviceIdType.MESH
f32, bf16 = jnp.float32, jnp.bfloat16

BLOCKS = 64
ROWS = 256
CHAN = 1024
SHARE = CHAN // BLOCKS
POINTS = 2 * BLOCKS * ROWS
GROUP = 4


def split_np(table):
    high = np.asarray(table, np.float32).astype(jnp.bfloat16)
    low = (np.asarray(table, np.float64) - high.astype(np.float64)).astype(jnp.bfloat16)
    return high, low


@functools.lru_cache(maxsize=None)
def fourier_tables():
    steps = np.arange(BLOCKS) + 0.5
    outer = 2 * np.pi * np.outer(steps, np.arange(BLOCKS)) / (2 * BLOCKS)
    block_forward = np.concatenate([np.cos(outer), -np.sin(outer)], axis=0)
    block_inverse = block_forward.T * (2.0 / POINTS)
    twist = 2 * np.pi * np.outer(steps, np.arange(ROWS)) / POINTS
    inner = 2 * np.pi * (np.outer(np.arange(ROWS), np.arange(ROWS)) % ROWS) / ROWS
    cos_in, sin_in = np.cos(inner), np.sin(inner)
    row_forward = np.block([[cos_in, -sin_in], [sin_in, cos_in]])
    row_inverse = np.block([[cos_in, sin_in], [-sin_in, cos_in]])
    return (
        np.concatenate(split_np(block_forward), axis=1),
        *split_np(block_inverse),
        np.cos(twist).astype(np.float32),
        np.sin(twist).astype(np.float32),
        np.stack(split_np(row_forward) + split_np(row_inverse)),
    )


def split(value):
    high = value.astype(bf16)
    return high, (value - high.astype(f32)).astype(bf16)


def dot(left, right):
    return jnp.dot(left, right, preferred_element_type=f32)


def dot_wide(left, right_high, right_low):
    high, low = split(left)
    return dot(high, right_high) + (dot(high, right_low) + dot(low, right_high))


def kernel(
    feat_far, filt_far, weight_far, row_far, taps, skip, bf, bi_hi, bi_lo, tw_cos, tw_sin,
    out,
    feat, filt, rows, halo, f_out, g_out, f_in, g_in, y_out, y_in,
    wide, spec, query, gated, w_all, hyena, acc,
    load_sems, greet_sems, halo_sems, f_sems, g_sems, y_sems, t_sems,
    z_send, z_recv, v_send, v_recv, u_send, u_recv, p_send, p_recv, h_send, h_recv,
):
    me = lax.axis_index("seq")
    col = lax.axis_index("ch")
    row = lax.div(me, 16)
    deep = lax.div(lax.rem(me, 16), 2)
    core = lax.rem(me, 2)

    def seq_at(r, d, c):
        return (r * 8 + d) * 2 + c

    def wrap(i, n):
        return lax.rem(i + n, n)

    def signal(sem, **where):
        pl.semaphore_signal(sem, inc=1, device_id=where, device_id_type=MESH)

    def remote(src, dst, send, recv, **where):
        return pltpu.make_async_remote_copy(
            src_ref=src, dst_ref=dst, send_sem=send, recv_sem=recv, device_id=where, device_id_type=MESH
        )

    barrier = pltpu.get_barrier_semaphore()
    after_me, before_me = lax.rem(me + 1, BLOCKS), wrap(me - 1, BLOCKS)
    mirror = {"seq": seq_at(col, deep, core), "ch": row}
    signal(barrier, seq=seq_at(row, deep, 1 - core))
    signal(barrier, seq=jnp.where(core == 0, before_me, after_me))
    for step in range(1, 8):
        signal(barrier, seq=seq_at(row, lax.rem(deep + step, 8), core))
    for step in range(1, 4):
        signal(barrier, seq=seq_at(lax.rem(row + step, 4), deep, core))
    for step in (1, 3):
        signal(barrier, ch=lax.rem(col + step, 4))

    @pl.when(row != col)
    def _():
        signal(barrier, **mirror)

    loads = [
        pltpu.make_async_copy(far, near, load_sems.at[i])
        for i, (far, near) in enumerate(((filt_far, filt), (feat_far, feat), (row_far, rows)))
    ]
    for load in loads:
        load.start()
    loads[0].wait()
    f_out[...] = filt[...].T.astype(bf16)

    pl.semaphore_wait(barrier, 14 + (row != col).astype(jnp.int32))

    halo_copy = remote(
        feat_far.at[:, pl.ds(ROWS - 16, 16), :], halo, halo_sems.at[0], halo_sems.at[1], seq=after_me
    )
    halo_copy.start()

    mirror_copy = remote(weight_far, w_all.at[col, deep, core], t_sems.at[0], t_sems.at[1], **mirror)
    same_copy = pltpu.make_async_copy(weight_far, w_all.at[row, deep, core], t_sems.at[1])

    @pl.when(row != col)
    def _():
        mirror_copy.start()

    @pl.when(row == col)
    def _():
        same_copy.start()

    for step in range(1, 4):
        signal(greet_sems.at[0], seq=seq_at(lax.rem(row + step, 4), deep, core))
    loads[1].wait()
    first = (me != 0).astype(f32)

    def mixed(b):
        middle = feat[b].astype(f32)
        back_one = pltpu.roll(middle, 1, 0)
        back_two = pltpu.roll(middle, 2, 0)
        return taps[b, 0:1] * middle + taps[b, 1:2] * back_one + taps[b, 2:3] * back_two

    def mixed_top(b):
        top = feat[b, 0:16].astype(f32)
        joined = jnp.concatenate([halo[b].astype(f32) * first, top], axis=0)
        back_one = pltpu.roll(joined, 1, 0)[16:]
        back_two = pltpu.roll(joined, 2, 0)[16:]
        return taps[b, 0:1] * top + taps[b, 1:2] * back_one + taps[b, 2:3] * back_two

    pl.semaphore_wait(greet_sems.at[0], 3)
    signal(greet_sems.at[1], seq=seq_at(row, deep, 1 - core))
    gated[...] = mixed(1) * mixed(2)
    pl.semaphore_wait(greet_sems.at[1], 1)

    def exchange(src, dst, sems):
        def send(k, carry):
            to = lax.rem(me + k * STRIDE, BLOCKS)
            remote(
                src.at[pl.ds(pl.multiple_of(to * SHARE, SHARE), SHARE)],
                dst.at[pl.ds(pl.multiple_of(me * SHARE, SHARE), SHARE)],
                sems.at[0], sems.at[1], seq=to,
            ).start()
            return carry

        lax.fori_loop(1, BLOCKS, send, 0)
        here = pl.ds(pl.multiple_of(me * SHARE, SHARE), SHARE)
        dst[here, :] = src[here, :]

    def exchanged(src, dst, sems):
        others = pl.ds(0, (BLOCKS - 1) * SHARE)
        pltpu.make_async_copy(src.at[others], dst.at[others], sems.at[1]).wait()
        pltpu.make_async_copy(src.at[others], dst.at[others], sems.at[0]).wait()

    exchange(f_out, f_in, f_sems)

    def z_copies(i):
        parts = (pl.ds(0, 64), pl.ds(0, 64)) if i < 3 else (pl.ds(0, 32), pl.ds(32, 32))
        up = w_all.at[row, wrap(deep - i, 8), core, parts[0]]
        down = w_all.at[row, lax.rem(deep + i, 8), core, parts[1]]
        return (
            remote(up, up, z_send.at[0, i], z_recv.at[0, i], seq=seq_at(row, lax.rem(deep + 1, 8), core)),
            remote(down, down, z_send.at[1, i], z_recv.at[1, i], seq=seq_at(row, lax.rem(deep + 7, 8), core)),
        )

    up_row, down_row = lax.rem(row + 1, 4), wrap(row - 1, 4)

    def v_copies(i):
        block = w_all.at[row, lax.rem(deep + i, 8), core]
        return (
            remote(block, block, v_send.at[0, i], v_recv.at[0, i], seq=seq_at(up_row, deep, core)),
            remote(block, block, v_send.at[1, i], v_recv.at[1, i], seq=seq_at(down_row, deep, core)),
        )

    def u_copy(i):
        source, to = (down_row, up_row) if i < 4 else (up_row, down_row)
        block = w_all.at[source, lax.rem(deep + i, 8), core]
        return remote(block, block, u_send.at[i], u_recv.at[i], seq=seq_at(to, deep, core))

    z_steps = [z_copies(i) for i in range(4)]
    v_steps = [v_copies(i) for i in range(8)]
    u_steps = [u_copy(i) for i in range(8)]

    def start(copies):
        for copy in copies:
            copy.start()

    def received(copies):
        for copy in copies:
            copy.wait_recv()

    @pl.when(row != col)
    def _():
        mirror_copy.wait()

    @pl.when(row == col)
    def _():
        same_copy.wait()

    start(z_steps[0])
    start(v_steps[0])

    halo_copy.wait()
    gated[0:16] = mixed_top(1) * mixed_top(2)
    g_out[...] = gated[...].T.astype(bf16)
    exchange(g_out, g_in, g_sems)
    query[...] = mixed(0)
    query[0:16] = mixed_top(0)

    for i in range(1, 4):
        received(z_steps[i - 1])
        start(z_steps[i])
        start(v_steps[i])
        start(v_steps[8 - i])
    received(z_steps[3])
    start(v_steps[4])

    def p_copy(i):
        ref = w_all.at[lax.rem(row + i, 4), :, core]
        return remote(ref, ref, p_send.at[i], p_recv.at[i], seq=seq_at(row, deep, 1 - core))

    p_copies = [p_copy(i) for i in range(4)]
    p_copies[0].start()

    def pass_on(i):
        if i < 4:
            v_steps[i][0].wait_recv()
        else:
            v_steps[i][1].wait_recv()
        u_steps[i].start()

    def widen(arrived):
        wide[0] = arrived[:, :128].astype(f32)
        wide[1] = arrived[:, 128:].astype(f32)

    def spectra(q):
        lines = []
        for c in range(GROUP):
            every = pl.ds(q * GROUP + c, BLOCKS, stride=SHARE)
            line = jnp.concatenate([wide[0, every, :], wide[1, every, :]], axis=1)
            both = dot(bf[...], jnp.concatenate([line, line], axis=0).astype(bf16))
            real, imag = both[:BLOCKS], both[BLOCKS:]
            lines.append(
                jnp.concatenate(
                    [
                        real * tw_cos[...] + imag * tw_sin[...],
                        imag * tw_cos[...] - real * tw_sin[...],
                    ],
                    axis=1,
                )
            )
        return dot_wide(jnp.concatenate(lines, axis=0), rows[0], rows[1])

    exchanged(f_out, f_in, f_sems)
    widen(f_in)
    loads[2].wait()

    def filter_group(q, carry):
        spec[q] = spectra(q)
        return carry

    lax.fori_loop(0, SHARE // GROUP, filter_group, 0)

    for i in (0, 1, 7, 2, 6):
        pass_on(i)

    exchanged(g_out, g_in, g_sems)
    widen(g_in)

    def conv_group(q, carry):
        spectrum = spectra(q)
        taps_spec = spec[q]
        sr, si = spectrum[:, :ROWS], spectrum[:, ROWS:]
        tr, ti = taps_spec[:, :ROWS], taps_spec[:, ROWS:]
        joint = jnp.concatenate([sr * tr - si * ti, sr * ti + si * tr], axis=1)
        back = dot_wide(joint, rows[2], rows[3])
        for c in range(GROUP):
            real = back[c * BLOCKS : (c + 1) * BLOCKS, :ROWS]
            imag = back[c * BLOCKS : (c + 1) * BLOCKS, ROWS:]
            both = jnp.concatenate(
                [
                    real * tw_cos[...] - imag * tw_sin[...],
                    imag * tw_cos[...] + real * tw_sin[...],
                ],
                axis=0,
            )
            high, low = split(both)
            series = dot(bi_hi[...], high) + (dot(bi_hi[...], low) + dot(bi_lo[...], high))
            every = pl.ds(q * GROUP + c, BLOCKS, stride=SHARE)
            wide[0, every, :] = series[:, :128]
            wide[1, every, :] = series[:, 128:]
        return carry

    lax.fori_loop(0, SHARE // GROUP, conv_group, 0)
    for half in range(2):
        y_out[half] = wide[half].astype(bf16)
        exchange(y_out.at[half], y_in.at[half], y_sems.at[half])

    for i in (3, 5, 4):
        pass_on(i)
    for i in range(8):
        if i < 4:
            v_steps[i][1].wait_recv()
        else:
            v_steps[i][0].wait_recv()
    p_copies[3].start()
    p_copies[1].start()

    left, right = wrap(col - 1, 4), lax.rem(col + 1, 4)

    def h_copies(half, passing):
        if passing:
            up = hyena.at[left, pl.ds(half * 128, 64)]
            down = hyena.at[right, pl.ds(half * 128 + 64, 64)]
        else:
            up = down = hyena.at[col, pl.ds(half * 128, 128)]
        i = 2 * passing + half
        return (
            remote(up, up, h_send.at[0, i], h_recv.at[0, i], ch=right),
            remote(down, down, h_send.at[1, i], h_recv.at[1, i], ch=left),
        )

    h_own = [h_copies(half, 0) for half in range(2)]
    h_far = [h_copies(half, 1) for half in range(2)]
    for half in range(2):
        exchanged(y_out.at[half], y_in.at[half], y_sems.at[half])
        part = slice(half * 128, half * 128 + 128)
        long_conv = y_in[half].astype(f32).T
        hyena[col, part] = (query[part] * (long_conv + skip[...] * gated[part])).astype(bf16)
        start(h_own[half])

    def project(source, half, fresh):
        part = slice(half * 128, half * 128 + 128)

        def tile(j, carry):
            cols = pl.ds(pl.multiple_of(j * 256, 256), 256)
            block = w_all[source, pl.ds(2 * j, 2)].reshape(256, CHAN)
            sums = lax.dot_general(
                hyena[source, part], block, (((1,), (1,)), ((), ())), preferred_element_type=f32
            )
            acc[part, cols] = sums if fresh else acc[part, cols] + sums
            return carry

        lax.fori_loop(0, 4, tile, 0)

    received(h_own[0])
    start(h_far[0])
    received(u_steps)
    p_copies[2].start()
    received(p_copies)
    project(col, 0, True)
    received(h_own[1])
    start(h_far[1])
    project(left, 0, False)
    project(right, 0, False)
    project(col, 1, True)
    received(h_far[0])
    project(lax.rem(col + 2, 4), 0, False)
    project(left, 1, False)
    project(right, 1, False)
    received(h_far[1])
    project(lax.rem(col + 2, 4), 1, False)
    out[...] = acc[...].astype(bf16)

    for copies in (*z_steps, *v_steps, u_steps, p_copies, *h_own, *h_far):
        for copy in copies:
            copy.wait_send()


STRIDE = 23


def shards(features, short_taps, filter_taps, skip_bias, out_weight):
    tables = [jnp.asarray(t) for t in fourier_tables()]
    near = pl.BlockSpec(memory_space=pltpu.VMEM)
    far = pl.BlockSpec(memory_space=pl.ANY)
    dma, vmem = pltpu.SemaphoreType.DMA, pltpu.VMEM
    return pl.pallas_call(
        kernel,
        out_shape=jax.ShapeDtypeStruct((ROWS, CHAN), bf16),
        in_specs=[far] * 4 + [near] * 7,
        out_specs=near,
        scratch_shapes=[
            vmem((3, ROWS, CHAN), bf16),
            vmem((ROWS, CHAN), f32),
            vmem((4, 2 * ROWS, 2 * ROWS), bf16),
            vmem((3, 16, CHAN), bf16),
            *[vmem((CHAN, ROWS), bf16)] * 4,
            *[vmem((2, CHAN, 128), bf16)] * 2,
            vmem((2, CHAN, 128), f32),
            vmem((SHARE // GROUP, GROUP * BLOCKS, 2 * ROWS), f32),
            vmem((ROWS, CHAN), f32),
            vmem((ROWS, CHAN), f32),
            vmem((4, 8, 2, 64, CHAN), bf16),
            vmem((4, ROWS, CHAN), bf16),
            vmem((ROWS, CHAN), f32),
            dma((3,)),
            pltpu.SemaphoreType.REGULAR((2,)),
            *[dma((2,))] * 3,
            dma((2, 2)),
            dma((2,)),
            *[dma((2, 4))] * 2,
            *[dma((2, 8))] * 2,
            *[dma((8,))] * 2,
            *[dma((4,))] * 2,
            *[dma((2, 4))] * 2,
        ],
        compiler_params=pltpu.CompilerParams(
            collective_id=0, has_side_effects=True, vmem_limit_bytes=60 * 1024 * 1024
        ),
    )(
        features, filter_taps, out_weight.T, tables[5],
        short_taps, skip_bias[None, :], *tables[:5],
    )


def solution(mesh):
    placed = (P(None, "seq", "ch"), P(None, None, "ch"), P("seq", "ch"), P("ch"), P("ch", "seq"))
    return jax.shard_map(
        shards, mesh=mesh, in_specs=placed, out_specs=P("seq", "ch"), check_vma=False
    )
```

time: 120 us -> 101 us (0.84)
  Pallas kernels: 116 us -> 99.1 us
  local copies, waits for them, and re-layouts: 3.61 us -> 1.87 us
    pallas_call x1, Pallas kernels: 116 us -> 99.1 us  [shards(): pl.pallas_call(kernel, out_shape=jax.ShapeDtypeStruct((ROWS, CHAN), bf16)...]
    unnamed x2 -> x1, local copies, waits for them, and re-layouts: 3.61 us -> 1.87 us
where the time goes in v2:
time: 101 us
  Pallas kernels  99.1 us (98%)
  local copies, waits for them, and re-layouts  1.87 us (2%)
    pallas_call x1, Pallas kernels, shards(): pl.pallas_call(kernel, out_shape=jax.ShapeDtypeStruct((ROWS, CHAN), bf16)...  99.1 us

profile of v2, /device:TPU:1, one launch (start us, length us, event | category | flops | bytes accessed | tf_op | source)
XLA Modules:
  0.0 101.0 jit_solution(6750251564731867242)
XLA Ops:
  0.0 99.1 %shard_map.109 = bf16[256,1024]{1,0:T(8,128)(2,1)} custom-call(bf16[3,256,1024]{2,1,0:T(8,128)(2,1)} %feat_far.1, f32[256,1024]{1,0:T(8,128)} %filt_far.1, bf16[64,1024]{1,0:T(8,128)(2,1)} %bitcast.2, bf16[4,512,512]{2,1,0:T(8,128)(2,1)} %constant.17.clone.row_far, f32[3,3,1024]{2,1,0:T(4,128)} %taps.1, f32[1,1024]{1,0:T(1,128)} %bitcast.3, ...), custom_call_target="tpu_custom_call" | custom-call | tf_op jit(solution)/shard_map/pallas_call | solution.py:399
  99.1 1.9 %copy.13 = bf16[256,1024]{1,0:T(8,128)(2,1)} copy(bf16[256,1024]{1,0:T(8,128)(2,1)} %shard_map.109) | data formatting | bytes 1048576

commit v3 on v2

--- a/solution.py
+++ b/solution.py
@@ -18,6 +18,7 @@
 SHARE = CHAN // BLOCKS
 POINTS = 2 * BLOCKS * ROWS
 GROUP = 4
+WAVE = CHAN // 2
 
 
 def split_np(table):
@@ -111,7 +112,13 @@
     for load in loads:
         load.start()
     loads[0].wait()
-    f_out[...] = filt[...].T.astype(bf16)
+
+    def packed(value, wave):
+        turned = value[:, wave * WAVE : (wave + 1) * WAVE].T
+        parts = [turned[:, h * 128 : (h + 1) * 128].reshape(BLOCKS, 8, 128) for h in range(2)]
+        return jnp.concatenate(parts, axis=1).reshape(CHAN, 128).astype(bf16)
+
+    f_out[0] = packed(filt[...], 0)
 
     pl.semaphore_wait(barrier, 14 + (row != col).astype(jnp.int32))
 
@@ -131,8 +138,43 @@
     def _():
         same_copy.start()
 
+    def share_to(src, dst, sems, to):
+        remote(
+            src.at[pl.ds(pl.multiple_of(to * SHARE, SHARE), SHARE)],
+            dst.at[pl.ds(pl.multiple_of(me * SHARE, SHARE), SHARE)],
+            sems.at[0], sems.at[1], seq=to,
+        ).start()
+
+    def exchange(src, dst, sems, begin=1, end=BLOCKS):
+        def send(k, carry):
+            share_to(src, dst, sems, lax.rem(me + k * STRIDE, BLOCKS))
+            return carry
+
+        lax.fori_loop(begin, end, send, 0)
+        if begin == 1:
+            here = pl.ds(pl.multiple_of(me * SHARE, SHARE), SHARE)
+            dst[here, :] = src[here, :]
+
     for step in range(1, 4):
         signal(greet_sems.at[0], seq=seq_at(lax.rem(row + step, 4), deep, core))
+
+    def to_line(k, carry):
+        share_to(f_out.at[0], f_in.at[0], f_sems.at[0], seq_at(row, lax.rem(deep + 3 * k, 8), core))
+        return carry
+
+    def to_core(k, carry):
+        near_by = seq_at(lax.rem(row + 1 + lax.rem(k, 3), 4), lax.rem(deep + 3 * k, 8), core)
+        share_to(f_out.at[0], f_in.at[0], f_sems.at[0], near_by)
+        return carry
+
+    def to_other(k, carry):
+        at = row * 8 + deep + 11 * k
+        share_to(f_out.at[0], f_in.at[0], f_sems.at[0], lax.rem(at, 32) * 2 + 1 - core)
+        return carry
+
+    lax.fori_loop(1, 8, to_line, 0)
+    here = pl.ds(pl.multiple_of(me * SHARE, SHARE), SHARE)
+    f_in[0, here, :] = f_out[0, here, :]
     loads[1].wait()
     first = (me != 0).astype(f32)
 
@@ -151,29 +193,14 @@
 
     pl.semaphore_wait(greet_sems.at[0], 3)
     signal(greet_sems.at[1], seq=seq_at(row, deep, 1 - core))
+    lax.fori_loop(0, 24, to_core, 0)
+    pl.semaphore_wait(greet_sems.at[1], 1)
     gated[...] = mixed(1) * mixed(2)
-    pl.semaphore_wait(greet_sems.at[1], 1)
-
-    def exchange(src, dst, sems):
-        def send(k, carry):
-            to = lax.rem(me + k * STRIDE, BLOCKS)
-            remote(
-                src.at[pl.ds(pl.multiple_of(to * SHARE, SHARE), SHARE)],
-                dst.at[pl.ds(pl.multiple_of(me * SHARE, SHARE), SHARE)],
-                sems.at[0], sems.at[1], seq=to,
-            ).start()
-            return carry
-
-        lax.fori_loop(1, BLOCKS, send, 0)
-        here = pl.ds(pl.multiple_of(me * SHARE, SHARE), SHARE)
-        dst[here, :] = src[here, :]
 
     def exchanged(src, dst, sems):
         others = pl.ds(0, (BLOCKS - 1) * SHARE)
         pltpu.make_async_copy(src.at[others], dst.at[others], sems.at[1]).wait()
         pltpu.make_async_copy(src.at[others], dst.at[others], sems.at[0]).wait()
-
-    exchange(f_out, f_in, f_sems)
 
     def z_copies(i):
         parts = (pl.ds(0, 64), pl.ds(0, 64)) if i < 3 else (pl.ds(0, 32), pl.ds(32, 32))
@@ -210,6 +237,39 @@
         for copy in copies:
             copy.wait_recv()
 
+    def p_copy(i, slot):
+        ref = w_all.at[lax.rem(row + i, 4), lax.rem(deep + slot, 8), core]
+        return remote(ref, ref, p_send.at[i, slot], p_recv.at[i, slot], seq=seq_at(row, deep, 1 - core))
+
+    p_copies = [[p_copy(i, slot) for slot in range(8)] for i in range(4)]
+
+    def spread(slot):
+        start(v_steps[slot])
+        p_copies[0][slot].start()
+
+    def take_lines(slot):
+        v_steps[slot][0].wait_recv()
+        if slot < 4:
+            u_steps[slot].start()
+        p_copies[3][slot].start()
+        v_steps[slot][1].wait_recv()
+        if slot >= 4:
+            u_steps[slot].start()
+        p_copies[1][slot].start()
+
+    lax.fori_loop(0, 32, to_other, 0)
+    f_out[1] = packed(filt[...], 1)
+
+    halo_copy.wait()
+    gated[0:16] = mixed_top(1) * mixed_top(2)
+    for wave in range(2):
+        g_out[wave] = packed(gated[...], wave)
+
+    def share(src, dst, sems, wave, begin=1, end=BLOCKS):
+        exchange(src.at[wave], dst.at[wave], sems.at[wave], begin, end)
+
+    share(g_out, g_in, g_sems, 0)
+
     @pl.when(row != col)
     def _():
         mirror_copy.wait()
@@ -219,46 +279,20 @@
         same_copy.wait()
 
     start(z_steps[0])
-    start(v_steps[0])
-
-    halo_copy.wait()
-    gated[0:16] = mixed_top(1) * mixed_top(2)
-    g_out[...] = gated[...].T.astype(bf16)
-    exchange(g_out, g_in, g_sems)
+    spread(0)
+    share(f_out, f_in, f_sems, 1)
     query[...] = mixed(0)
     query[0:16] = mixed_top(0)
-
-    for i in range(1, 4):
-        received(z_steps[i - 1])
-        start(z_steps[i])
-        start(v_steps[i])
-        start(v_steps[8 - i])
-    received(z_steps[3])
-    start(v_steps[4])
-
-    def p_copy(i):
-        ref = w_all.at[lax.rem(row + i, 4), :, core]
-        return remote(ref, ref, p_send.at[i], p_recv.at[i], seq=seq_at(row, deep, 1 - core))
-
-    p_copies = [p_copy(i) for i in range(4)]
-    p_copies[0].start()
-
-    def pass_on(i):
-        if i < 4:
-            v_steps[i][0].wait_recv()
-        else:
-            v_steps[i][1].wait_recv()
-        u_steps[i].start()
-
-    def widen(arrived):
-        wide[0] = arrived[:, :128].astype(f32)
-        wide[1] = arrived[:, 128:].astype(f32)
-
-    def spectra(q):
+    received(z_steps[0])
+    start(z_steps[1])
+    spread(1)
+    spread(7)
+    share(g_out, g_in, g_sems, 1)
+
+    def spectra(wave, q):
         lines = []
         for c in range(GROUP):
-            every = pl.ds(q * GROUP + c, BLOCKS, stride=SHARE)
-            line = jnp.concatenate([wide[0, every, :], wide[1, every, :]], axis=1)
+            line = jnp.concatenate([wide[wave, every, :] for every in every_block(q, c)], axis=1)
             both = dot(bf[...], jnp.concatenate([line, line], axis=0).astype(bf16))
             real, imag = both[:BLOCKS], both[BLOCKS:]
             lines.append(
@@ -272,123 +306,147 @@
             )
         return dot_wide(jnp.concatenate(lines, axis=0), rows[0], rows[1])
 
-    exchanged(f_out, f_in, f_sems)
-    widen(f_in)
+    def every_block(q, c):
+        return [pl.ds(q * GROUP + c + 8 * h, BLOCKS, stride=SHARE) for h in range(2)]
+
+    def filter_wave(wave):
+        exchanged(f_out.at[wave], f_in.at[wave], f_sems.at[wave])
+        wide[wave] = f_in[wave].astype(f32)
+
+        def filter_group(q, carry):
+            spec[2 * wave + q] = spectra(wave, q)
+            return carry
+
+        lax.fori_loop(0, 2, filter_group, 0)
+
+    def conv_wave(wave):
+        exchanged(g_out.at[wave], g_in.at[wave], g_sems.at[wave])
+        wide[wave] = g_in[wave].astype(f32)
+
+        def conv_group(q, carry):
+            spectrum = spectra(wave, q)
+            taps_spec = spec[2 * wave + q]
+            sr, si = spectrum[:, :ROWS], spectrum[:, ROWS:]
+            tr, ti = taps_spec[:, :ROWS], taps_spec[:, ROWS:]
+            joint = jnp.concatenate([sr * tr - si * ti, sr * ti + si * tr], axis=1)
+            back = dot_wide(joint, rows[2], rows[3])
+            for c in range(GROUP):
+                real = back[c * BLOCKS : (c + 1) * BLOCKS, :ROWS]
+                imag = back[c * BLOCKS : (c + 1) * BLOCKS, ROWS:]
+                both = jnp.concatenate(
+                    [
+                        real * tw_cos[...] - imag * tw_sin[...],
+                        imag * tw_cos[...] + real * tw_sin[...],
+                    ],
+                    axis=0,
+                )
+                high, low = split(both)
+                series = dot(bi_hi[...], high) + (dot(bi_hi[...], low) + dot(bi_lo[...], high))
+                for h, every in enumerate(every_block(q, c)):
+                    wide[wave, every, :] = series[:, h * 128 : (h + 1) * 128]
+            return carry
+
+        lax.fori_loop(0, 2, conv_group, 0)
+        y_out[wave] = wide[wave].astype(bf16)
+        share(y_out, y_in, y_sems, wave)
+
     loads[2].wait()
-
-    def filter_group(q, carry):
-        spec[q] = spectra(q)
-        return carry
-
-    lax.fori_loop(0, SHARE // GROUP, filter_group, 0)
-
-    for i in (0, 1, 7, 2, 6):
-        pass_on(i)
-
-    exchanged(g_out, g_in, g_sems)
-    widen(g_in)
-
-    def conv_group(q, carry):
-        spectrum = spectra(q)
-        taps_spec = spec[q]
-        sr, si = spectrum[:, :ROWS], spectrum[:, ROWS:]
-        tr, ti = taps_spec[:, :ROWS], taps_spec[:, ROWS:]
-        joint = jnp.concatenate([sr * tr - si * ti, sr * ti + si * tr], axis=1)
-        back = dot_wide(joint, rows[2], rows[3])
-        for c in range(GROUP):
-            real = back[c * BLOCKS : (c + 1) * BLOCKS, :ROWS]
-            imag = back[c * BLOCKS : (c + 1) * BLOCKS, ROWS:]
-            both = jnp.concatenate(
-                [
-                    real * tw_cos[...] - imag * tw_sin[...],
-                    imag * tw_cos[...] + real * tw_sin[...],
-                ],
-                axis=0,
-            )
-            high, low = split(both)
-            series = dot(bi_hi[...], high) + (dot(bi_hi[...], low) + dot(bi_lo[...], high))
-            every = pl.ds(q * GROUP + c, BLOCKS, stride=SHARE)
-            wide[0, every, :] = series[:, :128]
-            wide[1, every, :] = series[:, 128:]
-        return carry
-
-    lax.fori_loop(0, SHARE // GROUP, conv_group, 0)
-    for half in range(2):
-        y_out[half] = wide[half].astype(bf16)
-        exchange(y_out.at[half], y_in.at[half], y_sems.at[half])
-
-    for i in (3, 5, 4):
-        pass_on(i)
-    for i in range(8):
-        if i < 4:
-            v_steps[i][1].wait_recv()
+    filter_wave(0)
+    received(z_steps[1])
+    start(z_steps[2])
+    spread(2)
+    spread(6)
+    conv_wave(0)
+    received(z_steps[2])
+    start(z_steps[3])
+    spread(3)
+    spread(5)
+    take_lines(0)
+    filter_wave(1)
+    received(z_steps[3])
+    spread(4)
+    for slot in EARLY:
+        take_lines(slot)
+    conv_wave(1)
+    for slot in MIDDLE:
+        take_lines(slot)
+
+    left, right = wrap(col - 1, 4), lax.rem(col + 1, 4)
+
+    def h_copies(wave, passing):
+        if passing:
+            up = hyena.at[left, wave, pl.ds(0, 128)]
+            down = hyena.at[right, wave, pl.ds(128, 128)]
         else:
-            v_steps[i][0].wait_recv()
-    p_copies[3].start()
-    p_copies[1].start()
-
-    left, right = wrap(col - 1, 4), lax.rem(col + 1, 4)
-
-    def h_copies(half, passing):
-        if passing:
-            up = hyena.at[left, pl.ds(half * 128, 64)]
-            down = hyena.at[right, pl.ds(half * 128 + 64, 64)]
-        else:
-            up = down = hyena.at[col, pl.ds(half * 128, 128)]
-        i = 2 * passing + half
+            up = down = hyena.at[col, wave]
+        i = 2 * passing + wave
         return (
             remote(up, up, h_send.at[0, i], h_recv.at[0, i], ch=right),
             remote(down, down, h_send.at[1, i], h_recv.at[1, i], ch=left),
         )
 
-    h_own = [h_copies(half, 0) for half in range(2)]
-    h_far = [h_copies(half, 1) for half in range(2)]
-    for half in range(2):
-        exchanged(y_out.at[half], y_in.at[half], y_sems.at[half])
-        part = slice(half * 128, half * 128 + 128)
-        long_conv = y_in[half].astype(f32).T
-        hyena[col, part] = (query[part] * (long_conv + skip[...] * gated[part])).astype(bf16)
-        start(h_own[half])
-
-    def project(source, half, fresh):
-        part = slice(half * 128, half * 128 + 128)
-
+    h_own = [h_copies(wave, 0) for wave in range(2)]
+    h_far = [h_copies(wave, 1) for wave in range(2)]
+
+    def finish(wave):
+        exchanged(y_out.at[wave], y_in.at[wave], y_sems.at[wave])
+        series = y_in[wave].astype(f32).reshape(BLOCKS, SHARE, 128)
+        lanes = slice(wave * WAVE, (wave + 1) * WAVE)
+        for h in range(2):
+            part = slice(h * 128, h * 128 + 128)
+            long_conv = series[:, 8 * h : 8 * h + 8].reshape(WAVE, 128).T
+            hyena[col, wave, part] = (
+                query[part, lanes] * (long_conv + skip[:, lanes] * gated[part, lanes])
+            ).astype(bf16)
+        start(h_own[wave])
+
+    def project(source, wave, fresh=False):
         def tile(j, carry):
             cols = pl.ds(pl.multiple_of(j * 256, 256), 256)
-            block = w_all[source, pl.ds(2 * j, 2)].reshape(256, CHAN)
+            block = w_all[source, pl.ds(2 * j, 2), :, :, wave * WAVE : (wave + 1) * WAVE]
             sums = lax.dot_general(
-                hyena[source, part], block, (((1,), (1,)), ((), ())), preferred_element_type=f32
+                hyena[source, wave], block.reshape(256, WAVE), (((1,), (1,)), ((), ())),
+                preferred_element_type=f32,
             )
-            acc[part, cols] = sums if fresh else acc[part, cols] + sums
+            acc[:, cols] = sums if fresh else acc[:, cols] + sums
             return carry
 
         lax.fori_loop(0, 4, tile, 0)
 
+    finish(0)
+    for slot in LATE[:-1]:
+        take_lines(slot)
     received(h_own[0])
     start(h_far[0])
-    received(u_steps)
-    p_copies[2].start()
-    received(p_copies)
+    finish(1)
+    for slot in LATE[-1:]:
+        take_lines(slot)
+    for slot in range(8):
+        u_steps[slot].wait_recv()
+        p_copies[2][slot].start()
+    for copies in p_copies:
+        received(copies)
     project(col, 0, True)
     received(h_own[1])
     start(h_far[1])
-    project(left, 0, False)
-    project(right, 0, False)
-    project(col, 1, True)
+    project(left, 0)
+    project(right, 0)
+    project(col, 1)
     received(h_far[0])
-    project(lax.rem(col + 2, 4), 0, False)
-    project(left, 1, False)
-    project(right, 1, False)
+    project(lax.rem(col + 2, 4), 0)
+    project(left, 1)
+    project(right, 1)
     received(h_far[1])
-    project(lax.rem(col + 2, 4), 1, False)
+    project(lax.rem(col + 2, 4), 1)
     out[...] = acc[...].astype(bf16)
 
-    for copies in (*z_steps, *v_steps, u_steps, p_copies, *h_own, *h_far):
+    for copies in (*z_steps, *v_steps, u_steps, *p_copies, *h_own, *h_far):
         for copy in copies:
             copy.wait_send()
 
 
 STRIDE = 23
+EARLY, MIDDLE, LATE = (1, 7), (2, 6), (3, 5, 4)
 
 
 def shards(features, short_taps, filter_taps, skip_bias, out_weight):
@@ -406,24 +464,23 @@
             vmem((ROWS, CHAN), f32),
             vmem((4, 2 * ROWS, 2 * ROWS), bf16),
             vmem((3, 16, CHAN), bf16),
-            *[vmem((CHAN, ROWS), bf16)] * 4,
-            *[vmem((2, CHAN, 128), bf16)] * 2,
+            *[vmem((2, CHAN, 128), bf16)] * 6,
             vmem((2, CHAN, 128), f32),
             vmem((SHARE // GROUP, GROUP * BLOCKS, 2 * ROWS), f32),
             vmem((ROWS, CHAN), f32),
             vmem((ROWS, CHAN), f32),
             vmem((4, 8, 2, 64, CHAN), bf16),
-            vmem((4, ROWS, CHAN), bf16),
+            vmem((4, 2, ROWS, WAVE), bf16),
             vmem((ROWS, CHAN), f32),
             dma((3,)),
             pltpu.SemaphoreType.REGULAR((2,)),
-            *[dma((2,))] * 3,
-            dma((2, 2)),
+            dma((2,)),
+            *[dma((2, 2))] * 3,
             dma((2,)),
             *[dma((2, 4))] * 2,
             *[dma((2, 8))] * 2,
             *[dma((8,))] * 2,
-            *[dma((4,))] * 2,
+            *[dma((4, 8))] * 2,
             *[dma((2, 4))] * 2,
         ],
         compiler_params=pltpu.CompilerParams(

time: 101 us -> 86.3 us (0.85)
  Pallas kernels: 99.1 us -> 84.3 us
    pallas_call x1, Pallas kernels: 99.1 us -> 84.3 us  [shards(): pl.pallas_call(kernel, out_shape=jax.ShapeDtypeStruct((ROWS, CHAN), bf16)...]
where the time goes in v3:
time: 86.3 us; the launch traced here: 86.2 us
  Pallas kernels  84.3 us (98%)
  local copies, waits for them, and re-layouts  1.87 us (2%)
    pallas_call x1, Pallas kernels, shards(): pl.pallas_call(kernel, out_shape=jax.ShapeDtypeStruct((ROWS, CHAN), bf16)...  84.3 us
    unnamed x1, local copies, waits for them, and re-layouts  1.87 us

profile of v3, /device:TPU:1, one launch (start us, length us, event | category | flops | bytes accessed | tf_op | source)
XLA Modules:
  0.0 86.2 jit_solution(15473479683172629537)
XLA Ops:
  0.0 84.3 %shard_map.109 = bf16[256,1024]{1,0:T(8,128)(2,1)} custom-call(bf16[3,256,1024]{2,1,0:T(8,128)(2,1)} %feat_far.1, f32[256,1024]{1,0:T(8,128)} %filt_far.1, bf16[64,1024]{1,0:T(8,128)(2,1)} %bitcast.2, bf16[4,512,512]{2,1,0:T(8,128)(2,1)} %constant.17.clone.row_far, f32[3,3,1024]{2,1,0:T(4,128)} %taps.1, f32[1,1024]{1,0:T(1,128)} %bitcast.3, ...), custom_call_target="tpu_custom_call" | custom-call | tf_op jit(solution)/shard_map/pallas_call | solution.py:457
  84.3 1.9 %copy.13 = bf16[256,1024]{1,0:T(8,128)(2,1)} copy(bf16[256,1024]{1,0:T(8,128)(2,1)} %shard_map.109) | data formatting | bytes 1048576

commit v4 on v3

--- a/solution.py
+++ b/solution.py
@@ -373,20 +373,23 @@
 
     left, right = wrap(col - 1, 4), lax.rem(col + 1, 4)
 
-    def h_copies(wave, passing):
-        if passing:
-            up = hyena.at[left, wave, pl.ds(0, 128)]
-            down = hyena.at[right, wave, pl.ds(128, 128)]
+    def h_copies(wave, step):
+        first_half, second_half = pl.ds(0, 128), pl.ds(128, 128)
+        if step == 0:
+            up, down = hyena.at[col, wave, first_half], hyena.at[col, wave, second_half]
+        elif step == 1:
+            up, down = hyena.at[col, wave, second_half], hyena.at[col, wave, first_half]
         else:
-            up = down = hyena.at[col, wave]
-        i = 2 * passing + wave
+            up, down = hyena.at[left, wave, first_half], hyena.at[right, wave, second_half]
+        i = 2 * step + wave
         return (
             remote(up, up, h_send.at[0, i], h_recv.at[0, i], ch=right),
             remote(down, down, h_send.at[1, i], h_recv.at[1, i], ch=left),
         )
 
     h_own = [h_copies(wave, 0) for wave in range(2)]
-    h_far = [h_copies(wave, 1) for wave in range(2)]
+    h_rest = [h_copies(wave, 1) for wave in range(2)]
+    h_far = [h_copies(wave, 2) for wave in range(2)]
 
     def finish(wave):
         exchanged(y_out.at[wave], y_in.at[wave], y_sems.at[wave])
@@ -399,6 +402,7 @@
                 query[part, lanes] * (long_conv + skip[:, lanes] * gated[part, lanes])
             ).astype(bf16)
         start(h_own[wave])
+        start(h_rest[wave])
 
     def project(source, wave, fresh=False):
         def tile(j, carry):
@@ -429,18 +433,20 @@
     project(col, 0, True)
     received(h_own[1])
     start(h_far[1])
+    received(h_rest[0])
     project(left, 0)
     project(right, 0)
     project(col, 1)
     received(h_far[0])
     project(lax.rem(col + 2, 4), 0)
+    received(h_rest[1])
     project(left, 1)
     project(right, 1)
     received(h_far[1])
     project(lax.rem(col + 2, 4), 1)
     out[...] = acc[...].astype(bf16)
 
-    for copies in (*z_steps, *v_steps, u_steps, *p_copies, *h_own, *h_far):
+    for copies in (*z_steps, *v_steps, u_steps, *p_copies, *h_own, *h_rest, *h_far):
         for copy in copies:
             copy.wait_send()
 
@@ -481,7 +487,7 @@
             *[dma((2, 8))] * 2,
             *[dma((8,))] * 2,
             *[dma((4, 8))] * 2,
-            *[dma((2, 4))] * 2,
+            *[dma((2, 6))] * 2,
         ],
         compiler_params=pltpu.CompilerParams(
             collective_id=0, has_side_effects=True, vmem_limit_bytes=60 * 1024 * 1024

time: 86.3 us -> 86.4 us (level)
  no operation moved by 1% of the time
where the time goes in v4:
time: 86.4 us; the launch traced here: 86.2 us
  Pallas kernels  84.3 us (98%)
  local copies, waits for them, and re-layouts  1.87 us (2%)
    pallas_call x1, Pallas kernels, shards(): pl.pallas_call(kernel, out_shape=jax.ShapeDtypeStruct((ROWS, CHAN), bf16)...  84.3 us
    unnamed x1, local copies, waits for them, and re-layouts  1.87 us

profile of v4, /device:TPU:1, one launch (start us, length us, event | category | flops | bytes accessed | tf_op | source)
XLA Modules:
  0.0 86.2 jit_solution(17157478503917803034)
XLA Ops:
  0.0 84.3 %shard_map.109 = bf16[256,1024]{1,0:T(8,128)(2,1)} custom-call(bf16[3,256,1024]{2,1,0:T(8,128)(2,1)} %feat_far.1, f32[256,1024]{1,0:T(8,128)} %filt_far.1, bf16[64,1024]{1,0:T(8,128)(2,1)} %bitcast.2, bf16[4,512,512]{2,1,0:T(8,128)(2,1)} %constant.17.clone.row_far, f32[3,3,1024]{2,1,0:T(4,128)} %taps.1, f32[1,1024]{1,0:T(1,128)} %bitcast.3, ...), custom_call_target="tpu_custom_call" | custom-call | tf_op jit(solution)/shard_map/pallas_call | solution.py:463
  84.3 1.9 %copy.13 = bf16[256,1024]{1,0:T(8,128)(2,1)} copy(bf16[256,1024]{1,0:T(8,128)(2,1)} %shard_map.109) | data formatting | bytes 1048576

commit v5 on v4

--- a/solution.py
+++ b/solution.py
@@ -428,11 +428,11 @@
     for slot in range(8):
         u_steps[slot].wait_recv()
         p_copies[2][slot].start()
+    received(h_own[1])
+    start(h_far[1])
     for copies in p_copies:
         received(copies)
     project(col, 0, True)
-    received(h_own[1])
-    start(h_far[1])
     received(h_rest[0])
     project(left, 0)
     project(right, 0)

time: 86.4 us -> 86.3 us (level)
  no operation moved by 1% of the time
where the time goes in v5:
time: 86.3 us; the launch traced here: 86.2 us
  Pallas kernels  84.3 us (98%)
  local copies, waits for them, and re-layouts  1.87 us (2%)
    pallas_call x1, Pallas kernels, shards(): pl.pallas_call(kernel, out_shape=jax.ShapeDtypeStruct((ROWS, CHAN), bf16)...  84.3 us
    unnamed x1, local copies, waits for them, and re-layouts  1.87 us

profile of v5, /device:TPU:1, one launch (start us, length us, event | category | flops | bytes accessed | tf_op | source)
XLA Modules:
  0.0 86.2 jit_solution(17872736012400347473)
XLA Ops:
  0.0 84.3 %shard_map.109 = bf16[256,1024]{1,0:T(8,128)(2,1)} custom-call(bf16[3,256,1024]{2,1,0:T(8,128)(2,1)} %feat_far.1, f32[256,1024]{1,0:T(8,128)} %filt_far.1, bf16[64,1024]{1,0:T(8,128)(2,1)} %bitcast.2, bf16[4,512,512]{2,1,0:T(8,128)(2,1)} %constant.17.clone.row_far, f32[3,3,1024]{2,1,0:T(4,128)} %taps.1, f32[1,1024]{1,0:T(1,128)} %bitcast.3, ...), custom_call_target="tpu_custom_call" | custom-call | tf_op jit(solution)/shard_map/pallas_call | solution.py:463
  84.3 1.9 %copy.13 = bf16[256,1024]{1,0:T(8,128)(2,1)} copy(bf16[256,1024]{1,0:T(8,128)(2,1)} %shard_map.109) | data formatting | bytes 1048576
